TPU v7x, 256 devices: a whole 4x4x8 slice. The times are simulated.
256 devices in a mesh: head: 4 (over x_hi, core), loop: 64 (over x_lo, y, z).
Axes of the slice: x: 4 (x_hi: 2, x_lo: 2; x = x_hi * 2 + x_lo), y: 4, z: 8, core: 2. Of those that a mesh axis runs over, the one named last changes fastest.
Arguments:
- prompt_query_rows: bfloat16 [8192, 4096], P('loop', 'head'), as said below
- prompt_key_rows: bfloat16 [8192, 512], P('loop', 'head'), as said below
- prompt_value_rows: bfloat16 [8192, 512], P('loop', 'head'), may hold values from -6 to 6
- tail_query_rows: bfloat16 [64, 64, 4096], P('loop', None, 'head'), as said below
- tail_key_rows: bfloat16 [64, 64, 512], P('loop', None, 'head'), as said below
- tail_value_rows: bfloat16 [64, 64, 512], P('loop', None, 'head'), may hold values from -6 to 6
- tail_len: int32 [64], P('loop'), may hold values from 1 to 64, as said below
- stretch_order: int32 [128], replicated, may hold values from 0 to 127, each once
- out_weight: bfloat16 [4096, 5120], P('head'), may hold values from -0.09375 to 0.09375
Outputs:
- prompt_out: bfloat16 [8192, 5120], P('loop', 'head')
- tail_out: bfloat16 [64, 64, 5120], P('loop', None, 'head')
Inputs may be any that keep to these rules, and one draw needn't show every extreme that they name: `prompt_query_rows`: prompt queries. `prompt_key_rows`: prompt keys. `tail_query_rows`: tail queries. `tail_key_rows`: tail keys. `tail_len`: at least one tail has all 64 slots valid. A permutation: stored block j holds the prompt positions stretch_order[j] * 64 to stretch_order[j] * 64 + 63 in order.
All inputs are finite; a program needn't handle non-finite values.
Results may differ from a plain program's by a relative error of at most 0.015.
Values may be sent and summed in bfloat16 or wider, within the bound.
A program may use at most 64 MiB of HBM per device.

v0:
```python
import math

import jax
import jax.numpy as jnp
from jax import lax
from jax.sharding import PartitionSpec as P

HEAD_SIZE = 128
CH = 64
TAIL_SLOTS = 64


NEGATIVE = -1e30


def lookup_stretches(rows, stretch_order):
    blocks = rows // CH
    table = jnp.arange(stretch_order.shape[0], dtype=jnp.int32)
    picked = jnp.sum(
        jnp.where(blocks[:, None] == table[None, :], stretch_order[None, :], 0), axis=1
    )
    return picked * CH + rows % CH


def attend_block(carry, queries, joined_keys, joined_values, visible):
    running_max, running_sum, weighted = carry
    scale = 1.0 / math.sqrt(queries.shape[-1])
    scores = (
        jnp.einsum("rkgd,nkd->kgrn", queries, joined_keys, preferred_element_type=jnp.float32)
        * scale
    )
    scores = jnp.where(visible[None, None], scores, NEGATIVE)
    fresh_max = jnp.maximum(running_max, jnp.max(scores, axis=-1))
    weights = jnp.where(visible[None, None], jnp.exp(scores - fresh_max[..., None]), 0.0)
    shrink = jnp.exp(running_max - fresh_max)
    running_sum = running_sum * shrink + jnp.sum(weights, axis=-1)
    weighted = weighted * shrink[..., None] + jnp.einsum(
        "kgrn,nkd->kgrd",
        weights.astype(jnp.bfloat16),
        joined_values,
        preferred_element_type=jnp.float32,
    )
    return (fresh_max, running_sum, weighted)


def on_device(
    prompt_query_rows,
    prompt_key_rows,
    prompt_value_rows,
    tail_query_rows,
    tail_key_rows,
    tail_value_rows,
    tail_len,
    stretch_order,
    out_weight,
):
    prompt_rows = prompt_query_rows.shape[0]
    samples = tail_query_rows.shape[0]
    kv_heads = prompt_key_rows.shape[1] // HEAD_SIZE
    query_groups = prompt_query_rows.shape[1] // prompt_key_rows.shape[1]
    prompt_len = stretch_order.shape[0] * CH
    tail_rows = samples * TAIL_SLOTS
    total_rows = prompt_rows + tail_rows
    queries = jnp.concatenate(
        [prompt_query_rows, tail_query_rows.reshape(tail_rows, -1)], axis=0
    ).reshape(total_rows, kv_heads, query_groups, HEAD_SIZE)
    own_rows = lax.axis_index("loop") * prompt_rows + jnp.arange(prompt_rows, dtype=jnp.int32)
    tail_steps = jnp.tile(jnp.arange(TAIL_SLOTS, dtype=jnp.int32), samples)
    sample_ids = jnp.repeat(jnp.arange(samples, dtype=jnp.int32), TAIL_SLOTS)
    query_pos = jnp.concatenate(
        [lookup_stretches(own_rows, stretch_order), prompt_len + tail_steps]
    )
    query_seg = jnp.concatenate([jnp.full((prompt_rows,), -1, jnp.int32), sample_ids])
    start_carry = (
        jnp.full((kv_heads, query_groups, total_rows), NEGATIVE, jnp.float32),
        jnp.zeros((kv_heads, query_groups, total_rows), jnp.float32),
        jnp.zeros((kv_heads, query_groups, total_rows, HEAD_SIZE), jnp.float32),
    )
    key_rows = lax.all_gather(prompt_key_rows, "loop", axis=0, tiled=True)
    value_rows = lax.all_gather(prompt_value_rows, "loop", axis=0, tiled=True)
    count = key_rows.shape[0]
    span = 512

    def inner(index, state):
        offset = index * span
        block_keys = lax.dynamic_slice_in_dim(key_rows, offset, span, 0).reshape(
            span, kv_heads, HEAD_SIZE
        )
        block_values = lax.dynamic_slice_in_dim(value_rows, offset, span, 0).reshape(
            span, kv_heads, HEAD_SIZE
        )
        key_pos = lookup_stretches(offset + jnp.arange(span, dtype=jnp.int32), stretch_order)
        visible = key_pos[None, :] <= query_pos[:, None]
        return attend_block(state, queries, block_keys, block_values, visible)

    carry = lax.fori_loop(0, count // span, inner, start_carry)
    limits = jnp.repeat(tail_len, TAIL_SLOTS)
    tail_valid = tail_steps < limits
    tail_visible = (
        ((prompt_len + tail_steps)[None, :] <= query_pos[:, None])
        & (sample_ids[None, :] == query_seg[:, None])
        & tail_valid[None, :]
    )
    tail_joined_keys = tail_key_rows.reshape(tail_rows, kv_heads, HEAD_SIZE)
    tail_joined_values = tail_value_rows.reshape(tail_rows, kv_heads, HEAD_SIZE)
    running_max, running_sum, weighted = attend_block(
        carry, queries, tail_joined_keys, tail_joined_values, tail_visible
    )
    mixed = weighted / running_sum[..., None]
    live_rows = jnp.concatenate([jnp.ones((prompt_rows,), bool), tail_valid])
    mixed = jnp.where(live_rows[None, None, :, None], mixed, 0.0)
    heads_out = jnp.transpose(mixed, (2, 0, 1, 3)).reshape(total_rows, -1).astype(jnp.bfloat16)
    partial_value = jnp.dot(heads_out, out_weight, preferred_element_type=jnp.float32)
    shares = lax.psum_scatter(
        partial_value.astype(jnp.bfloat16), "head", scatter_dimension=1, tiled=True
    ).astype(jnp.float32)
    shares = shares.astype(jnp.bfloat16)
    return (shares[:prompt_rows], shares[prompt_rows:].reshape(samples, TAIL_SLOTS, -1))


def solution(mesh):
    placed = (
        P("loop", "head"),
        P("loop", "head"),
        P("loop", "head"),
        P("loop", None, "head"),
        P("loop", None, "head"),
        P("loop", None, "head"),
        P("loop"),
        P(),
        P("head", None),
    )
    return jax.shard_map(
        on_device,
        mesh=mesh,
        in_specs=placed,
        out_specs=(P("loop", "head"), P("loop", None, "head")),
        check_vma=False,
    )
```

profile of v0, /device:TPU:1, one launch (start us, length us, event | category | flops | bytes accessed | tf_op | source)
XLA Modules:
  0.0 777.1 jit_solution(5959595670335695058)
XLA Ops:
  8.8 1.0 copy.34
  9.8 0.9 copy.35
  13.9 1.9 fusion.49
  15.8 253.7 %all-gather.3.cloned.1.call-done = bf16[8192,128]{1,0:T(8,128)(2,1)} async-done(((bf16[128,128]{1,0:T(8,128)(2,1)}), bf16[8192,128]{1,0:T(8,128)(2,1)}) %all-gather.3.cloned.1.call-update) | async-done | bytes 2097168 | tf_op jit(solution)/shard_map/all_gather | solution.py:79
  269.5 299.0 %all-gather.5.cloned.1.call-done = bf16[8192,128]{1,0:T(8,128)(2,1)} async-done(((bf16[128,128]{1,0:T(8,128)(2,1)}), bf16[8192,128]{1,0:T(8,128)(2,1)}) %all-gather.5.cloned.1.call-update) | async-done | bytes 2097168 | tf_op jit(solution)/shard_map/all_gather | solution.py:80
  568.6 103.1 %while.20 = (s32[]{:T(128)}, f32[1,8,192]{2,1,0:T(8,128)S(1)}, f32[1,8,192]{2,1,0:T(8,128)S(1)}, f32[1,8,192,128]{3,2,1,0:T(8,128)}, s32[128]{0:T(128)S(1)}, /*i...) while((s32[]{:T(128)}, f32[1,8,192]{2,1,0:T(8,128)S(1)}, ...), condition=%wide.region_5.6_spmd.clone, body=%wide.region_1.5_spmd.clone.sunk | while | flops 413785600 | bytes 18462216 | solution.py:96
  569.0 1.8 fusion.61
  570.8 1.1 fusion.63
  571.9 2.2 fusion.64
  575.4 1.8 fusion.61
  577.2 1.1 fusion.63
  578.4 2.2 fusion.64
  580.5 0.9 copy-done.3
  581.8 1.8 fusion.61
  583.7 1.1 fusion.63
  584.8 2.2 fusion.64
  587.0 0.9 copy-done.3
  588.3 1.8 fusion.61
  590.1 1.1 fusion.63
  591.3 2.2 fusion.64
  593.4 0.9 copy-done.3
  594.7 1.8 fusion.61
  596.6 1.1 fusion.63
  597.7 2.2 fusion.64
  601.2 1.8 fusion.61
  603.0 1.1 fusion.63
  604.1 2.2 fusion.64
  606.3 0.9 copy-done.3
  607.6 1.8 fusion.61
  609.5 1.1 fusion.63
  610.6 2.2 fusion.64
  614.1 1.8 fusion.61
  615.9 1.1 fusion.63
  617.0 2.2 fusion.64
  620.5 1.8 fusion.61
  622.3 1.1 fusion.63
  623.5 2.2 fusion.64
  626.9 1.8 fusion.61
  628.8 1.1 fusion.63
  629.9 2.2 fusion.64
  633.4 1.8 fusion.61
  635.2 1.1 fusion.63
  636.4 2.2 fusion.64
  639.8 1.8 fusion.61
  641.7 1.1 fusion.63
  642.8 2.2 fusion.64
  646.3 1.8 fusion.61
  648.1 1.1 fusion.63
  649.2 2.2 fusion.64
  652.7 1.8 fusion.61
  654.6 1.1 fusion.63
  655.7 2.2 fusion.64
  659.2 1.8 fusion.61
  661.0 1.1 fusion.63
  662.1 2.2 fusion.64
  665.6 1.8 fusion.61
  667.4 1.1 fusion.63
  668.6 2.2 fusion.64
  671.9 1.6 fusion.36
  673.7 1.7 fusion.35
  675.6 7.5 convolution_convert_fusion
  683.1 84.1 %reduce-scatter.2.cloned.1.call-done = bf16[192,1280]{1,0:T(8,128)(2,1)} async-done(((bf16[192,5120]{1,0:T(8,128)(2,1)}), bf16[192,1280]{1,0:T(8,128)(2,1)}) %reduce-scatter.2.cloned.1.call-update) | async-done | bytes 491536 | tf_op jit(solution)/shard_map/reduce_scatter | solution.py:114
  767.3 1.7 slice.8
  769.0 1.6 slice_bitcast_fusion
  (203 shorter events, 22.1 us)
Async XLA Ops:
  7.2 666.5 %copy-start = (bf16[1,64,128]{2,1,0:T(8,128)(2,1)S(1)}, bf16[1,64,128]{2,1,0:T(8,128)(2,1)}, u32[]{:S(2)}) copy-start(bf16[1,64,128]{2,1,0:T(8,128)(2,1)} %param.16) | copy-start | bytes 49156
  7.2 561.4 %copy-start.1 = (s32[128]{0:T(128)S(1)}, s32[128]{0:T(128)}, u32[]{:S(2)}) copy-start(s32[128]{0:T(128)} %param.18) | copy-start | bytes 1540
  7.2 262.3 %all-gather.3.cloned.1.call-start = ((), (), s32[]{:S(2)}) async-start(), calls=%async_computation.1 | async-start | bytes 2129920 | tf_op jit(solution)/shard_map/all_gather | solution.py:79
  7.9 560.6 %all-gather.5.cloned.1.call-start = ((), (), s32[]{:S(2)}) async-start(), calls=%async_computation.2 | async-start | bytes 2129920 | tf_op jit(solution)/shard_map/all_gather | solution.py:80
  8.7 758.6 %reduce-scatter.2.cloned.1.call-start = ((), (), s32[]{:S(2)}) async-start(), calls=%async_computation.3 | async-start | bytes 2457600 | tf_op jit(solution)/shard_map/reduce_scatter | solution.py:114
  570.8 1.1 copy-start.2
  574.1 0.9 copy-start.3
  577.2 1.1 copy-start.2
  580.5 0.9 copy-start.3
  583.7 1.1 copy-start.2
  587.0 0.9 copy-start.3
  590.1 1.1 copy-start.2
  593.4 0.9 copy-start.3
  596.5 1.1 copy-start.2
  599.9 0.9 copy-start.3
  603.0 1.1 copy-start.2
  606.3 0.9 copy-start.3
  609.4 1.1 copy-start.2
  612.7 0.9 copy-start.3
  615.9 1.1 copy-start.2
  619.2 0.9 copy-start.3
  622.3 1.1 copy-start.2
  625.6 0.9 copy-start.3
  628.8 1.1 copy-start.2
  632.1 0.9 copy-start.3
  635.2 1.1 copy-start.2
  638.5 0.9 copy-start.3
  641.6 1.1 copy-start.2
  645.0 0.9 copy-start.3
  648.1 1.1 copy-start.2
  651.4 0.9 copy-start.3
  654.5 1.1 copy-start.2
  657.8 0.9 copy-start.3
  661.0 1.1 copy-start.2
  664.3 0.9 copy-start.3
  667.4 1.1 copy-start.2
  670.7 0.9 copy-start.3
Sparse Core Ops, SparseCore 0:
  9.8 259.6 all-gather.2
  271.3 297.2 all-gather.4
  683.2 83.9 reduce-scatter.1
where the time goes:
time: 779 us; the launch traced here: 777 us
  waiting for transfers between devices  638 us (82%)
  matrix products  74.5 us (10%)
  other arithmetic  27.4 us (4%)
  local copies, waits for them, and re-layouts  21.2 us (3%)
  between operations  14.6 us (2%)
    all_gather x1, waiting for transfers between devices, on_device(): value_rows = lax.all_gather(prompt_value_rows, 'loop', axis=0, tiled=True)  299 us
    all_gather x1, waiting for transfers between devices, on_device(): key_rows = lax.all_gather(prompt_key_rows, 'loop', axis=0, tiled=True)  254 us
    reduce_scatter x1, waiting for transfers between devices, on_device(): lax.psum_scatter(partial_value.astype(jnp.bfloat16), 'head', scatter_dime...  84.1 us
    dot_general x17, matrix products, attend_block(): jnp.einsum('kgrn,nkd->kgrd', weights.astype(jnp.bfloat16), joined_values,...  36.1 us
    dot_general x17, matrix products, attend_block(): jnp.einsum('rkgd,nkd->kgrn', queries, joined_keys, preferred_element_type...  30.9 us
    reduce_sum x17, other arithmetic, attend_block(): running_sum = running_sum * shrink + jnp.sum(weights, axis=-1)  19.1 us
  transfers between devices with their start and end apart: 3, of which 3 were waited for; matrix products, arithmetic and copies ran while one was open for 1% of the time, Pallas kernels for 0%

commit v1 on v0

v1 whole, which is shorter than its diff:
```python
import functools
import math

import jax
import jax.numpy as jnp
from jax import lax
from jax.experimental import pallas as pl
from jax.experimental.pallas import tpu as pltpu
from jax.sharding import PartitionSpec as P

F32, BF16 = jnp.float32, jnp.bfloat16
MESH = pl.DeviceIdType.MESH
NT = (((1,), (1,)), ((), ()))
HIDDEN = -1e30
RATE = math.log2(math.e) / math.sqrt(128.0)
STEPS = (0, 1, -1, 2, -2, 3, -3, 4)
PLACE = {0: 0, 1: 1, -1: 2, 2: 3, -2: 4, 3: 5, -3: 6, 4: 7, -4: 7}
BATCHES = ((0, 1), (1, 3), (3, 5), (5, 8))
LINES = (0, 1, -1, 2)


def kernel(
    pq, pk, pv, tq, tk, tv, tail_len, order, weight,
    prompt_out, tail_out,
    kv, q, tkv, hot, wv, qs, acc, top, mixed, mine, half_out, half_in, kept, cross_out, cross_in,
    send_sem, recv_sem, local_sem,
):
    head, loop = lax.axis_index("head"), lax.axis_index("loop")
    xh, c = head // 2, head % 2
    xl, y, z = loop // 32, (loop // 8) % 4, loop % 8
    guest = c != xl

    def device(xh_=xh, c_=c, xl_=xl, y_=y, z_=z):
        return (xh_ * 2 + c_, (xl_ * 4 + y_) * 8 + z_)

    sibling = device(c_=1 - c)
    partner = device(c_=1 - c, xl_=1 - xl)
    across = device(xh_=1 - xh)
    up, down = device(y_=(y + 1) % 4), device(y_=(y + 3) % 4)
    along = {k: device(z_=(z + k + 8) % 8) for k in (1, -1, 2, -2, 3, -3, 4)}

    started = []

    def remote(src, dst, to):
        n = len(started)
        copy = pltpu.make_async_remote_copy(
            src_ref=src, dst_ref=dst, send_sem=send_sem.at[n], recv_sem=recv_sem.at[n],
            device_id=to, device_id_type=MESH,
        )
        started.append(copy)
        return copy

    def send(src, dst, to):
        copy = remote(src, dst, to)
        copy.start()
        return copy

    weight_copies = []
    for j, (d, e) in enumerate(((0, 0), (1, 0), (0, 1), (1, 1))):
        block = (xh + d) % 2 * 2 + (c + e) % 2
        weight_copies.append(pltpu.make_async_copy(
            weight.at[:, pl.ds(pl.multiple_of(block * 1280, 1280), 1280)], wv.at[j], local_sem.at[j]))

    moves = (
        (pk, kv.at[0, 0, 0, 0]),
        (pv, kv.at[1, 0, 0, 0]),
        (tk, tkv.at[0, pl.ds(0, 64)]),
        (tv, tkv.at[1, pl.ds(0, 64)]),
        (pq, q.at[pl.ds(0, 128)]),
        (tq, q.at[pl.ds(128, 64)]),
    )
    here = [pltpu.make_async_copy(s, d, local_sem.at[4 + i]) for i, (s, d) in enumerate(moves)]
    there = [remote(s, d, partner) for s, d in moves]

    barrier = pltpu.get_barrier_semaphore()
    friends = [sibling, partner, across, up, down] + list(along.values())
    for friend in friends:
        pl.semaphore_signal(barrier, inc=1, device_id=friend, device_id_type=MESH)

    @pl.when(jnp.logical_not(guest))
    def _():
        for copy in here:
            copy.start()

    for copy in weight_copies:
        copy.start()

    row = lax.broadcasted_iota(jnp.int32, (128, 128), 0)
    col = lax.broadcasted_iota(jnp.int32, (128, 128), 1)
    shifted = col - (row >= 64).astype(jnp.int32)
    for i, dy in enumerate(LINES):
        for p, dz in enumerate(STEPS):
            for rr in range(2):
                r = (c + rr) % 2
                block = 2 * ((r * 4 + (y + dy + 4) % 4) * 8 + (z + dz + 8) % 8)
                hot[i, p, rr] = jnp.where(shifted == block, 1.0, 0.0).astype(BF16)

    tkv[:, pl.ds(64, 64), :] = jnp.zeros((2, 64, 128), BF16)

    lane = lax.broadcasted_iota(jnp.int32, (1, 128), 1)
    first = 2 * ((c * 4 + y) * 8 + z)
    ranks = order[...]
    for g in range(3):
        if g < 2:
            own = jnp.sum(jnp.where(lane == first + g, ranks, 0), axis=1, keepdims=True)
            seen = jnp.where(ranks < own, 0.0, HIDDEN)
        else:
            seen = jnp.zeros((1, 128), F32)
        for h in range(2):
            qs[2 * g + h, :, 128:] = jnp.broadcast_to(seen, (256, 128)).astype(BF16)

    pl.semaphore_wait(barrier, len(friends))

    @pl.when(guest)
    def _():
        for copy in there:
            copy.start()

    def arrived(numbers):
        @pl.when(guest)
        def _():
            for n in numbers:
                there[n].wait_recv()

        @pl.when(jnp.logical_not(guest))
        def _():
            for n in numbers:
                here[n].wait()

    arrived((0, 1))

    def shards(i, batch, rr, part=None):
        lo, hi = BATCHES[batch]
        part = slice(None) if part is None else part
        return kv.at[part, i, pl.ds(lo, hi - lo), rr]

    sib, ups, downs, far = {}, {}, {}, {}

    def to_sibling(i, b):
        sib[i, b] = send(shards(i, b, 0), shards(i, b, 1), sibling)

    def to_lines(b):
        ups[b] = send(shards(0, b, 0), shards(2, b, 0), up)
        downs[b] = send(shards(0, b, 0), shards(1, b, 0), down)

    def pass_on(b):
        far[0, b] = send(shards(1, b, 0, 0), shards(3, b, 0, 0), down)
        far[1, b] = send(shards(2, b, 0, 1), shards(3, b, 0, 1), up)

    zs = {}

    def to_z(k):
        zs[k] = send(kv.at[:, 0, 0, 0], kv.at[:, 0, PLACE[-k], 0], along[k])

    to_z(1)
    to_z(-1)
    to_sibling(0, 0)
    to_lines(0)
    for k in (2, -2, 3, -3, 4):
        to_z(k)

    arrived((2, 3, 4, 5))
    for t in range(6):
        g, h = t // 2, t % 2
        for e in range(4):
            qs[t, e * 64:(e + 1) * 64, :128] = q[g * 64:(g + 1) * 64, (h * 4 + e) * 128:(h * 4 + e + 1) * 128]

    ones = jnp.ones((128, 128), BF16)
    slot = lax.broadcasted_iota(jnp.int32, (256, 128), 0) % 64
    key = lax.broadcasted_iota(jnp.int32, (256, 128), 1)
    early = (key < 64) & (key <= slot)
    late = (key >= 64) & (key - 64 <= slot)
    for t in range(6):
        g = t // 2
        keys, values = (kv[0, 0, 0, 0], kv[1, 0, 0, 0]) if g < 2 else (tkv[0], tkv[1])
        s = lax.dot_general(qs[t, :, :128], keys, NT, preferred_element_type=F32)
        s = jnp.where(late if g == 1 else early, s, HIDDEN)
        peak = jnp.max(s, axis=1, keepdims=True)
        w = jnp.exp2((s - peak) * RATE).astype(BF16)
        acc[t] = jnp.dot(w, jnp.concatenate([values, ones], axis=1), preferred_element_type=F32)
        top[t] = jnp.broadcast_to(peak, (256, 128))

    def attend(i, lo, hi, t):
        n = (hi - lo) * 256
        keys = kv[0, i, lo:hi].reshape(n, 128)
        values = kv[1, i, lo:hi].reshape(n, 128)
        marks = hot[i, lo:hi].reshape(n, 128)
        s = lax.dot_general(
            qs[t], jnp.concatenate([keys, marks], axis=1), NT, preferred_element_type=F32)
        old = top[t]
        new = jnp.maximum(old, jnp.max(s, axis=1, keepdims=True))
        w = jnp.exp2((s - new[:, :1]) * RATE).astype(BF16)
        shrink = jnp.exp2((old - new) * RATE)
        top[t] = new
        add = jnp.dot(
            w, jnp.concatenate([values, jnp.ones((n, 128), BF16)], axis=1), preferred_element_type=F32)
        acc[t] = acc[t] * shrink[:, :1] + add

    def attend_all(i, lo, hi):
        @pl.loop(0, 3)
        def _(g):
            for h in range(2):
                attend(i, lo, hi, 2 * g + h)

    zs[1].wait_recv()
    zs[-1].wait_recv()
    to_lines(1)
    to_sibling(0, 1)
    sib[0, 0].wait_recv()
    zs[2].wait_recv()
    zs[-2].wait_recv()
    to_lines(2)
    to_sibling(0, 2)
    sib[0, 1].wait_recv()
    attend_all(0, 0, 3)
    for b in (0, 1):
        ups[b].wait_recv()
        downs[b].wait_recv()
        pass_on(b)
        to_sibling(1, b)
        to_sibling(2, b)
    sib[0, 2].wait_recv()
    attend_all(0, 3, 5)
    for k in (3, -3, 4):
        zs[k].wait_recv()
    to_lines(3)
    to_sibling(0, 3)
    ups[2].wait_recv()
    downs[2].wait_recv()
    pass_on(2)
    to_sibling(1, 2)
    to_sibling(2, 2)
    sib[0, 3].wait_recv()
    attend_all(0, 5, 8)
    for b in (0, 1, 2):
        sib[1, b].wait_recv()
    attend_all(1, 0, 5)
    for b in (0, 1, 2):
        far[0, b].wait_recv()
        far[1, b].wait_recv()
        to_sibling(3, b)
    ups[3].wait_recv()
    downs[3].wait_recv()
    pass_on(3)
    to_sibling(1, 3)
    to_sibling(2, 3)
    for b in (0, 1, 2):
        sib[2, b].wait_recv()
    attend_all(2, 0, 5)
    far[0, 3].wait_recv()
    far[1, 3].wait_recv()
    to_sibling(3, 3)
    for i in (1, 2):
        sib[i, 3].wait_recv()
    for b in range(4):
        sib[3, b].wait_recv()

    for copy in weight_copies:
        copy.wait()

    back, core, over = {}, {}, {}

    def finish(g):
        for h in range(2):
            t = 2 * g + h
            attend(1, 5, 8, t)
            attend(2, 5, 8, t)
            attend(3, 0, 8, t)
            out = (acc[t, :, :128] / acc[t, :, 128:]).astype(BF16)
            for e in range(4):
                mixed[g, h, :, e * 128:(e + 1) * 128] = out[e * 64:(e + 1) * 64]
            back[g, h] = remote(mixed.at[g, h], mine.at[g, h], partner)

            @pl.when(guest)
            def _():
                back[g, h].start()

            @pl.when(jnp.logical_not(guest))
            def _():
                mine[g, h] = mixed[g, h]

    def project(g):
        @pl.when(guest)
        def _():
            for h in range(2):
                back[g, h].wait_recv()

        lefts, rights = mine[g, 0], mine[g, 1]
        if g == 2:
            live = lax.broadcasted_iota(jnp.int32, (64, 512), 0) < tail_len[0]
            lefts = jnp.where(live, lefts, jnp.zeros_like(lefts))
            rights = jnp.where(live, rights, jnp.zeros_like(rights))
        rows = jnp.concatenate([lefts, rights], axis=1)
        for j in (3, 2, 1, 0):
            for n in range(5):
                part = jnp.dot(rows, wv[j, :, n * 256:(n + 1) * 256], preferred_element_type=F32)
                if j >= 2:
                    half_out[g, j - 2, :, n * 256:(n + 1) * 256] = part.astype(BF16)
                else:
                    kept[g, j, :, n * 256:(n + 1) * 256] = part
            if j == 2:
                core[g] = send(half_out.at[g], half_in.at[g], sibling)

    def cross(g):
        core[g].wait_recv()
        cross_out[g] = (kept[g, 1] + half_in[g, 1].astype(F32)).astype(BF16)
        over[g] = send(cross_out.at[g], cross_in.at[g], across)

    def close(g):
        over[g].wait_recv()
        out = kept[g, 0] + half_in[g, 0].astype(F32) + cross_in[g].astype(F32)
        if g < 2:
            prompt_out[g * 64:(g + 1) * 64] = out.astype(BF16)
        else:
            tail_out[...] = out.astype(BF16)

    finish(0)
    finish(1)
    project(0)
    finish(2)
    cross(0)
    project(1)
    cross(1)
    project(2)
    cross(2)
    close(0)
    close(1)
    close(2)

    lone = list(there) + list(back.values())
    for copy in started:
        if not any(copy is other for other in lone):
            copy.wait_send()

    @pl.when(guest)
    def _():
        for copy in lone:
            copy.wait_send()


COPIES = 6 + 7 + 16 + 8 + 8 + 6 + 3 + 3


def on_device(pq, pk, pv, tq, tk, tv, tail_len, order, weight):
    vmem, hbm = pl.BlockSpec(memory_space=pltpu.VMEM), pl.BlockSpec(memory_space=pl.ANY)
    prompt, tail = pl.pallas_call(
        kernel,
        out_shape=(jax.ShapeDtypeStruct((128, 1280), BF16), jax.ShapeDtypeStruct((64, 1280), BF16)),
        in_specs=[hbm] * 6 + [pl.BlockSpec(memory_space=pltpu.SMEM), vmem, hbm],
        out_specs=(vmem, vmem),
        scratch_shapes=[
            pltpu.VMEM((2, 4, 8, 2, 128, 128), BF16),
            pltpu.VMEM((192, 1024), BF16),
            pltpu.VMEM((2, 128, 128), BF16),
            pltpu.VMEM((4, 8, 2, 128, 128), BF16),
            pltpu.VMEM((4, 1024, 1280), BF16),
            pltpu.VMEM((6, 256, 256), BF16),
            pltpu.VMEM((6, 256, 256), F32),
            pltpu.VMEM((6, 256, 128), F32),
            pltpu.VMEM((3, 2, 64, 512), BF16),
            pltpu.VMEM((3, 2, 64, 512), BF16),
            pltpu.VMEM((3, 2, 64, 1280), BF16),
            pltpu.VMEM((3, 2, 64, 1280), BF16),
            pltpu.VMEM((3, 2, 64, 1280), F32),
            pltpu.VMEM((3, 64, 1280), BF16),
            pltpu.VMEM((3, 64, 1280), BF16),
            pltpu.SemaphoreType.DMA((COPIES,)),
            pltpu.SemaphoreType.DMA((COPIES,)),
            pltpu.SemaphoreType.DMA((10,)),
        ],
        compiler_params=pltpu.CompilerParams(
            collective_id=0, has_side_effects=True, vmem_limit_bytes=56 << 20
        ),
    )(pq, pk, pv, tq.reshape(64, 1024), tk.reshape(64, 128), tv.reshape(64, 128),
      tail_len, order.reshape(1, 128), weight)
    return prompt, tail.reshape(1, 64, 1280)


def solution(mesh):
    placed = (
        P("loop", "head"),
        P("loop", "head"),
        P("loop", "head"),
        P("loop", None, "head"),
        P("loop", None, "head"),
        P("loop", None, "head"),
        P("loop"),
        P(),
        P("head", None),
    )
    return jax.shard_map(
        on_device,
        mesh=mesh,
        in_specs=placed,
        out_specs=(P("loop", "head"), P("loop", None, "head")),
        check_vma=False,
    )
```

time: 779 us -> 80.5 us (0.10)
  waiting for transfers between devices: 638 us -> 0 us
  Pallas kernels: 0 us -> 75.7 us
  matrix products: 74.5 us -> 0 us
  other arithmetic: 27.4 us -> 0 us
  local copies, waits for them, and re-layouts: 21.2 us -> 3.31 us
  between operations: 14.6 us -> 1.29 us
    all_gather x2 -> x0, waiting for transfers between devices: 553 us -> none  [the longest x1 299 us: on_device(): value_rows = lax.all_gather(prompt_value_rows, 'loop', axis=0, tiled=True)]
    reduce_scatter x1 -> x0, waiting for transfers between devices: 84.1 us -> none  [on_device(): lax.psum_scatter(partial_value.astype(jnp.bfloat16), 'head', scatter_dime...]
    pallas_call x0 -> x1, Pallas kernels: none -> 75.7 us  [on_device(): pl.pallas_call(kernel, out_shape=(jax.ShapeDtypeStruct((128, 1280), BF16)...]
    dot_general x35 -> x0, matrix products: 74.5 us -> none  [the longest x17 36.1 us: attend_block(): jnp.einsum('kgrn,nkd->kgrd', weights.astype(jnp.bfloat16), joined_values,...]
    reduce_sum x34 -> x0, other arithmetic: 23.7 us -> none  [the longest x17 19.1 us: attend_block(): running_sum = running_sum * shrink + jnp.sum(weights, axis=-1)]
    while x82 -> x0, local copies, waits for them, and re-layouts: 14.7 us -> none
  transfers between devices with their start and end apart: 3 -> 0, of which waited for: 3 -> 0; matrix products, arithmetic and copies ran while one was open for 1% -> 0% of each run, Pallas kernels for 0% -> 0%
where the time goes in v1:
time: 80.5 us; the launch traced here: 80.3 us
  Pallas kernels  75.7 us (94%)
  local copies, waits for them, and re-layouts  3.31 us (4%)
  between operations  1.29 us (2%)
    pallas_call x1, Pallas kernels, on_device(): pl.pallas_call(kernel, out_shape=(jax.ShapeDtypeStruct((128, 1280), BF16)...  75.7 us
    unnamed x2, local copies, waits for them, and re-layouts  3.31 us

profile of v1, /device:TPU:1, one launch (start us, length us, event | category | flops | bytes accessed | tf_op | source)
XLA Modules:
  0.0 80.3 jit_solution(2417852072886985374)
XLA Ops:
  1.3 75.7 %shard_map.104 = (bf16[128,1280]{1,0:T(8,128)(2,1)}, bf16[64,1280]{1,0:T(8,128)(2,1)}) custom-call(bf16[128,1024]{1,0:T(8,128)(2,1)} %pq.1, bf16[128,128]{1,0:T(8,128)(2,1)} %pk.1, bf16[128,128]{1,0:T(8,128)(2,1)} %pv.1, bf16[64,1024]{1,0:T(8,128)(2,1)} %bitcast.6, bf16[64,128]{1,0:T(8,128)(2,1)} %bitcast.7, bf16[64,128]{1,0:T(8,128)(2,1)} %bitcast.8, ...), custom_call_target="tpu_custom_call" | custom-call | tf_op jit(solution)/shard_map/pallas_call | solution.py:346
  77.0 1.7 %copy.14 = bf16[128,1280]{1,0:T(8,128)(2,1)} copy(bf16[128,1280]{1,0:T(8,128)(2,1)} %get-tuple-element.8) | data formatting | bytes 655360
  78.7 1.6 %copy.15 = bf16[1,64,1280]{2,1,0:T(8,128)(2,1)} copy(bf16[1,64,1280]{2,1,0:T(8,128)(2,1)} %bitcast.5) | data formatting | bytes 327680

commit v2 on v1

--- a/solution.py
+++ b/solution.py
@@ -15,7 +15,7 @@
 RATE = math.log2(math.e) / math.sqrt(128.0)
 STEPS = (0, 1, -1, 2, -2, 3, -3, 4)
 PLACE = {0: 0, 1: 1, -1: 2, 2: 3, -2: 4, 3: 5, -3: 6, 4: 7, -4: 7}
-BATCHES = ((0, 1), (1, 3), (3, 5), (5, 8))
+BATCHES = ((0, 1), (1, 3), (3, 5), (5, 7), (7, 8))
 LINES = (0, 1, -1, 2)
 
 
@@ -37,7 +37,8 @@
     partner = device(c_=1 - c, xl_=1 - xl)
     across = device(xh_=1 - xh)
     up, down = device(y_=(y + 1) % 4), device(y_=(y + 3) % 4)
-    along = {k: device(z_=(z + k + 8) % 8) for k in (1, -1, 2, -2, 3, -3, 4)}
+    along = {k: device(z_=(z + k + 8) % 8) for k in (1, -1, 2, -2)}
+    beyond = device(y_=(y + 2) % 4)
 
     started = []
 
@@ -66,14 +67,15 @@
         (pv, kv.at[1, 0, 0, 0]),
         (tk, tkv.at[0, pl.ds(0, 64)]),
         (tv, tkv.at[1, pl.ds(0, 64)]),
-        (pq, q.at[pl.ds(0, 128)]),
         (tq, q.at[pl.ds(128, 64)]),
+        (pq.at[pl.ds(0, 64)], q.at[pl.ds(0, 64)]),
+        (pq.at[pl.ds(64, 64)], q.at[pl.ds(64, 64)]),
     )
     here = [pltpu.make_async_copy(s, d, local_sem.at[4 + i]) for i, (s, d) in enumerate(moves)]
     there = [remote(s, d, partner) for s, d in moves]
 
     barrier = pltpu.get_barrier_semaphore()
-    friends = [sibling, partner, across, up, down] + list(along.values())
+    friends = [sibling, partner, across, up, down, beyond] + list(along.values())
     for friend in friends:
         pl.semaphore_signal(barrier, inc=1, device_id=friend, device_id_type=MESH)
 
@@ -134,7 +136,7 @@
         part = slice(None) if part is None else part
         return kv.at[part, i, pl.ds(lo, hi - lo), rr]
 
-    sib, ups, downs, far = {}, {}, {}, {}
+    sib, ups, downs, zs = {}, {}, {}, {}
 
     def to_sibling(i, b):
         sib[i, b] = send(shards(i, b, 0), shards(i, b, 1), sibling)
@@ -143,117 +145,136 @@
         ups[b] = send(shards(0, b, 0), shards(2, b, 0), up)
         downs[b] = send(shards(0, b, 0), shards(1, b, 0), down)
 
-    def pass_on(b):
-        far[0, b] = send(shards(1, b, 0, 0), shards(3, b, 0, 0), down)
-        far[1, b] = send(shards(2, b, 0, 1), shards(3, b, 0, 1), up)
-
-    zs = {}
-
-    def to_z(k):
-        zs[k] = send(kv.at[:, 0, 0, 0], kv.at[:, 0, PLACE[-k], 0], along[k])
-
-    to_z(1)
-    to_z(-1)
+    def to_z(i, k):
+        zs[i, k] = send(kv.at[:, i, 0, 0], kv.at[:, i, PLACE[-k], 0], along[k])
+
+    def pass_on(i):
+        for k in (1, -1):
+            come = PLACE[-2 * k]
+            zs[i, 3 * k] = send(kv.at[:, i, come, 0], kv.at[:, i, PLACE[-3 * k], 0], along[k])
+        for k in (1, -1):
+            come, part = PLACE[-2 * k], (1 - k) // 2
+            zs[i, 4 * k] = send(kv.at[part, i, come, 0], kv.at[part, i, 7, 0], along[2 * k])
+
+    def got_z(i, *ks):
+        for k in ks:
+            zs[i, k].wait_recv()
+            zs[i, -k].wait_recv()
+
+    def got_lines(b):
+        ups[b].wait_recv()
+        downs[b].wait_recv()
+        to_sibling(1, b)
+        to_sibling(2, b)
+
+    def got_sibling(i, *bs):
+        for b in bs:
+            sib[i, b].wait_recv()
+
+    to_z(0, 1)
+    to_z(0, -1)
     to_sibling(0, 0)
     to_lines(0)
-    for k in (2, -2, 3, -3, 4):
-        to_z(k)
-
-    arrived((2, 3, 4, 5))
-    for t in range(6):
-        g, h = t // 2, t % 2
-        for e in range(4):
-            qs[t, e * 64:(e + 1) * 64, :128] = q[g * 64:(g + 1) * 64, (h * 4 + e) * 128:(h * 4 + e + 1) * 128]
+    own_far = send(kv.at[:, 0, 0, 0], kv.at[:, 3, 0, 0], beyond)
+    to_z(0, 2)
+    to_z(0, -2)
 
     ones = jnp.ones((128, 128), BF16)
     slot = lax.broadcasted_iota(jnp.int32, (256, 128), 0) % 64
     key = lax.broadcasted_iota(jnp.int32, (256, 128), 1)
     early = (key < 64) & (key <= slot)
     late = (key >= 64) & (key - 64 <= slot)
-    for t in range(6):
-        g = t // 2
-        keys, values = (kv[0, 0, 0, 0], kv[1, 0, 0, 0]) if g < 2 else (tkv[0], tkv[1])
-        s = lax.dot_general(qs[t, :, :128], keys, NT, preferred_element_type=F32)
-        s = jnp.where(late if g == 1 else early, s, HIDDEN)
-        peak = jnp.max(s, axis=1, keepdims=True)
-        w = jnp.exp2((s - peak) * RATE).astype(BF16)
-        acc[t] = jnp.dot(w, jnp.concatenate([values, ones], axis=1), preferred_element_type=F32)
-        top[t] = jnp.broadcast_to(peak, (256, 128))
-
-    def attend(i, lo, hi, t):
+
+    def begin(g):
+        for h in range(2):
+            t = 2 * g + h
+            for e in range(4):
+                qs[t, e * 64:(e + 1) * 64, :128] = q[g * 64:(g + 1) * 64, (h * 4 + e) * 128:(h * 4 + e + 1) * 128]
+            keys, values = (kv[0, 0, 0, 0], kv[1, 0, 0, 0]) if g < 2 else (tkv[0], tkv[1])
+            s = lax.dot_general(qs[t, :, :128], keys, NT, preferred_element_type=F32)
+            s = jnp.where(late if g == 1 else early, s, HIDDEN)
+            peak = jnp.max(s, axis=1, keepdims=True)
+            w = jnp.exp2((s - peak) * RATE).astype(BF16)
+            acc[t] = jnp.dot(w, jnp.concatenate([values, ones], axis=1), preferred_element_type=F32)
+            top[t] = jnp.broadcast_to(peak, (256, 128))
+
+    def scores(i, lo, hi, t):
         n = (hi - lo) * 256
         keys = kv[0, i, lo:hi].reshape(n, 128)
-        values = kv[1, i, lo:hi].reshape(n, 128)
         marks = hot[i, lo:hi].reshape(n, 128)
-        s = lax.dot_general(
+        return lax.dot_general(
             qs[t], jnp.concatenate([keys, marks], axis=1), NT, preferred_element_type=F32)
-        old = top[t]
-        new = jnp.maximum(old, jnp.max(s, axis=1, keepdims=True))
-        w = jnp.exp2((s - new[:, :1]) * RATE).astype(BF16)
-        shrink = jnp.exp2((old - new) * RATE)
-        top[t] = new
-        add = jnp.dot(
-            w, jnp.concatenate([values, jnp.ones((n, 128), BF16)], axis=1), preferred_element_type=F32)
-        acc[t] = acc[t] * shrink[:, :1] + add
+
+    def attend(steps):
+        ready = scores(*steps[0])
+        for at, (i, lo, hi, t) in enumerate(steps):
+            s = ready
+            if at + 1 < len(steps):
+                ready = scores(*steps[at + 1])
+            n = (hi - lo) * 256
+            values = kv[1, i, lo:hi].reshape(n, 128)
+            old = top[t]
+            new = jnp.maximum(old, jnp.max(s, axis=1, keepdims=True))
+            w = jnp.exp2((s - new[:, :1]) * RATE).astype(BF16)
+            shrink = jnp.exp2((old - new) * RATE)
+            top[t] = new
+            add = jnp.dot(
+                w, jnp.concatenate([values, jnp.ones((n, 128), BF16)], axis=1), preferred_element_type=F32)
+            acc[t] = acc[t] * shrink[:, :1] + add
 
     def attend_all(i, lo, hi):
-        @pl.loop(0, 3)
-        def _(g):
-            for h in range(2):
-                attend(i, lo, hi, 2 * g + h)
-
-    zs[1].wait_recv()
-    zs[-1].wait_recv()
+        attend([(i, lo, hi, t) for t in range(6)])
+
+    arrived((2, 3, 4))
+    begin(2)
+    got_z(0, 1)
     to_lines(1)
     to_sibling(0, 1)
-    sib[0, 0].wait_recv()
-    zs[2].wait_recv()
-    zs[-2].wait_recv()
+    own_far.wait_recv()
+    for k in (1, -1, 2, -2):
+        to_z(3, k)
+    to_sibling(3, 0)
+    arrived((5,))
+    begin(0)
+    arrived((6,))
+    begin(1)
+    got_z(0, 2)
+    pass_on(0)
     to_lines(2)
     to_sibling(0, 2)
-    sib[0, 1].wait_recv()
+    got_lines(0)
+    got_lines(1)
+    got_sibling(0, 0, 1)
     attend_all(0, 0, 3)
-    for b in (0, 1):
-        ups[b].wait_recv()
-        downs[b].wait_recv()
-        pass_on(b)
-        to_sibling(1, b)
-        to_sibling(2, b)
-    sib[0, 2].wait_recv()
-    attend_all(0, 3, 5)
-    for k in (3, -3, 4):
-        zs[k].wait_recv()
+    got_z(3, 1)
+    to_sibling(3, 1)
+    got_z(0, 3)
     to_lines(3)
     to_sibling(0, 3)
-    ups[2].wait_recv()
-    downs[2].wait_recv()
-    pass_on(2)
-    to_sibling(1, 2)
-    to_sibling(2, 2)
-    sib[0, 3].wait_recv()
-    attend_all(0, 5, 8)
-    for b in (0, 1, 2):
-        sib[1, b].wait_recv()
+    got_z(3, 2)
+    pass_on(3)
+    to_sibling(3, 2)
+    got_z(0, 4)
+    to_lines(4)
+    to_sibling(0, 4)
+    got_lines(2)
+    got_sibling(1, 0, 1, 2)
     attend_all(1, 0, 5)
-    for b in (0, 1, 2):
-        far[0, b].wait_recv()
-        far[1, b].wait_recv()
-        to_sibling(3, b)
-    ups[3].wait_recv()
-    downs[3].wait_recv()
-    pass_on(3)
-    to_sibling(1, 3)
-    to_sibling(2, 3)
-    for b in (0, 1, 2):
-        sib[2, b].wait_recv()
+    got_lines(3)
+    got_z(3, 3)
+    to_sibling(3, 3)
+    got_sibling(2, 0, 1, 2)
     attend_all(2, 0, 5)
-    far[0, 3].wait_recv()
-    far[1, 3].wait_recv()
-    to_sibling(3, 3)
+    got_lines(4)
+    got_z(3, 4)
+    to_sibling(3, 4)
+    got_sibling(0, 2, 3, 4)
+    attend_all(0, 3, 8)
+    got_sibling(3, 0, 1, 2)
+    attend_all(3, 0, 5)
     for i in (1, 2):
-        sib[i, 3].wait_recv()
-    for b in range(4):
-        sib[3, b].wait_recv()
+        got_sibling(i, 3, 4)
+    got_sibling(3, 3, 4)
 
     for copy in weight_copies:
         copy.wait()
@@ -261,11 +282,9 @@
     back, core, over = {}, {}, {}
 
     def finish(g):
+        attend([(i, lo, hi, 2 * g + h) for i, lo, hi in ((1, 5, 8), (2, 5, 8), (3, 5, 8)) for h in range(2)])
         for h in range(2):
             t = 2 * g + h
-            attend(1, 5, 8, t)
-            attend(2, 5, 8, t)
-            attend(3, 0, 8, t)
             out = (acc[t, :, :128] / acc[t, :, 128:]).astype(BF16)
             for e in range(4):
                 mixed[g, h, :, e * 128:(e + 1) * 128] = out[e * 64:(e + 1) * 64]
@@ -338,7 +357,12 @@
             copy.wait_send()
 
 
-COPIES = 6 + 7 + 16 + 8 + 8 + 6 + 3 + 3
+COPIES = 7 + 8 + 8 + 1 + 10 + 20 + 6 + 3 + 3
+
+
+def hand_over(prompt, tail, prompt_out, tail_out):
+    prompt_out[...] = prompt[...]
+    tail_out[...] = tail[...]
 
 
 def on_device(pq, pk, pv, tq, tk, tv, tail_len, order, weight):
@@ -366,14 +390,19 @@
             pltpu.VMEM((3, 64, 1280), BF16),
             pltpu.SemaphoreType.DMA((COPIES,)),
             pltpu.SemaphoreType.DMA((COPIES,)),
-            pltpu.SemaphoreType.DMA((10,)),
+            pltpu.SemaphoreType.DMA((11,)),
         ],
         compiler_params=pltpu.CompilerParams(
             collective_id=0, has_side_effects=True, vmem_limit_bytes=56 << 20
         ),
     )(pq, pk, pv, tq.reshape(64, 1024), tk.reshape(64, 128), tv.reshape(64, 128),
       tail_len, order.reshape(1, 128), weight)
-    return prompt, tail.reshape(1, 64, 1280)
+    return pl.pallas_call(
+        hand_over,
+        out_shape=(jax.ShapeDtypeStruct((128, 1280), BF16), jax.ShapeDtypeStruct((1, 64, 1280), BF16)),
+        in_specs=[vmem, vmem],
+        out_specs=(vmem, vmem),
+    )(prompt, tail.reshape(1, 64, 1280))
 
 
 def solution(mesh):

time: 80.5 us -> 67.4 us (0.84)
  Pallas kernels: 75.7 us -> 66 us
  local copies, waits for them, and re-layouts: 3.31 us -> 0 us
    pallas_call x1, Pallas kernels: 75.7 us -> 64.2 us  [on_device(): pl.pallas_call(kernel, out_shape=(jax.ShapeDtypeStruct((128, 1280), BF16)...]
    unnamed x2 -> x0, local copies, waits for them, and re-layouts: 3.31 us -> none
    pallas_call x0 -> x1, Pallas kernels: none -> 1.81 us  [on_device(): pl.pallas_call(hand_over, out_shape=(jax.ShapeDtypeStruct((128, 1280), BF...]
where the time goes in v2:
time: 67.4 us; the launch traced here: 67.3 us
  Pallas kernels  66 us (98%)
  between operations  1.29 us (2%)
    pallas_call x1, Pallas kernels, on_device(): pl.pallas_call(kernel, out_shape=(jax.ShapeDtypeStruct((128, 1280), BF16)...  64.2 us
    pallas_call x1, Pallas kernels, on_device(): pl.pallas_call(hand_over, out_shape=(jax.ShapeDtypeStruct((128, 1280), BF...  1.81 us

profile of v2, /device:TPU:1, one launch (start us, length us, event | category | flops | bytes accessed | tf_op | source)
XLA Modules:
  0.0 67.3 jit_solution(8940384541659835576)
XLA Ops:
  1.3 64.2 %shard_map.104 = (bf16[128,1280]{1,0:T(8,128)(2,1)}, bf16[64,1280]{1,0:T(8,128)(2,1)}) custom-call(bf16[128,1024]{1,0:T(8,128)(2,1)} %pq.1, bf16[128,128]{1,0:T(8,128)(2,1)} %pk.1, bf16[128,128]{1,0:T(8,128)(2,1)} %pv.1, bf16[64,1024]{1,0:T(8,128)(2,1)} %bitcast.6, bf16[64,128]{1,0:T(8,128)(2,1)} %bitcast.7, bf16[64,128]{1,0:T(8,128)(2,1)} %bitcast.8, ...), custom_call_target="tpu_custom_call" | custom-call | tf_op jit(solution)/shard_map/pallas_call | solution.py:370
  65.5 1.8 %shard_map.105 = (bf16[128,1280]{1,0:T(8,128)(2,1)}, bf16[1,64,1280]{2,1,0:T(8,128)(2,1)}) custom-call(bf16[128,1280]{1,0:T(8,128)(2,1)} %get-tuple-element.4.prompt, bf16[1,64,1280]{2,1,0:T(8,128)(2,1)} %bitcast.5), custom_call_target="tpu_custom_call" | custom-call | tf_op jit(solution)/shard_map/pallas_call | solution.py:400

commit v3 on v2

--- a/solution.py
+++ b/solution.py
@@ -298,27 +298,32 @@
             def _():
                 mine[g, h] = mixed[g, h]
 
-    def project(g):
-        @pl.when(guest)
-        def _():
-            for h in range(2):
-                back[g, h].wait_recv()
-
-        lefts, rights = mine[g, 0], mine[g, 1]
-        if g == 2:
-            live = lax.broadcasted_iota(jnp.int32, (64, 512), 0) < tail_len[0]
-            lefts = jnp.where(live, lefts, jnp.zeros_like(lefts))
-            rights = jnp.where(live, rights, jnp.zeros_like(rights))
-        rows = jnp.concatenate([lefts, rights], axis=1)
+    def project(*groups):
+        blocks = []
+        for g in groups:
+            @pl.when(guest)
+            def _():
+                for h in range(2):
+                    back[g, h].wait_recv()
+
+            block = jnp.concatenate([mine[g, 0], mine[g, 1]], axis=1)
+            if g == 2:
+                live = lax.broadcasted_iota(jnp.int32, (64, 1024), 0) < tail_len[0]
+                block = jnp.where(live, block, jnp.zeros_like(block))
+            blocks.append(block)
+        rows = blocks[0] if len(blocks) == 1 else jnp.concatenate(blocks, axis=0)
         for j in (3, 2, 1, 0):
             for n in range(5):
                 part = jnp.dot(rows, wv[j, :, n * 256:(n + 1) * 256], preferred_element_type=F32)
-                if j >= 2:
-                    half_out[g, j - 2, :, n * 256:(n + 1) * 256] = part.astype(BF16)
-                else:
-                    kept[g, j, :, n * 256:(n + 1) * 256] = part
+                for at, g in enumerate(groups):
+                    piece = part[at * 64:(at + 1) * 64]
+                    if j >= 2:
+                        half_out[g, j - 2, :, n * 256:(n + 1) * 256] = piece.astype(BF16)
+                    else:
+                        kept[g, j, :, n * 256:(n + 1) * 256] = piece
             if j == 2:
-                core[g] = send(half_out.at[g], half_in.at[g], sibling)
+                for g in groups:
+                    core[g] = send(half_out.at[g], half_in.at[g], sibling)
 
     def cross(g):
         core[g].wait_recv()
@@ -335,10 +340,9 @@
 
     finish(0)
     finish(1)
-    project(0)
     finish(2)
+    project(0, 1)
     cross(0)
-    project(1)
     cross(1)
     project(2)
     cross(2)

time: 67.4 us -> 66.1 us (0.981)
  Pallas kernels: 66 us -> 64.7 us
    pallas_call x1, Pallas kernels: 64.2 us -> 62.9 us  [on_device(): pl.pallas_call(kernel, out_shape=(jax.ShapeDtypeStruct((128, 1280), BF16)...]
where the time goes in v3:
time: 66.1 us; the launch traced here: 66 us
  Pallas kernels  64.7 us (98%)
  between operations  1.29 us (2%)
    pallas_call x1, Pallas kernels, on_device(): pl.pallas_call(kernel, out_shape=(jax.ShapeDtypeStruct((128, 1280), BF16)...  62.9 us
    pallas_call x1, Pallas kernels, on_device(): pl.pallas_call(hand_over, out_shape=(jax.ShapeDtypeStruct((128, 1280), BF...  1.81 us

profile of v3, /device:TPU:1, one launch (start us, length us, event | category | flops | bytes accessed | tf_op | source)
XLA Modules:
  0.0 66.0 jit_solution(6189662817569859052)
XLA Ops:
  1.3 62.9 %shard_map.104 = (bf16[128,1280]{1,0:T(8,128)(2,1)}, bf16[64,1280]{1,0:T(8,128)(2,1)}) custom-call(bf16[128,1024]{1,0:T(8,128)(2,1)} %pq.1, bf16[128,128]{1,0:T(8,128)(2,1)} %pk.1, bf16[128,128]{1,0:T(8,128)(2,1)} %pv.1, bf16[64,1024]{1,0:T(8,128)(2,1)} %bitcast.6, bf16[64,128]{1,0:T(8,128)(2,1)} %bitcast.7, bf16[64,128]{1,0:T(8,128)(2,1)} %bitcast.8, ...), custom_call_target="tpu_custom_call" | custom-call | tf_op jit(solution)/shard_map/pallas_call | solution.py:374
  64.2 1.8 %shard_map.105 = (bf16[128,1280]{1,0:T(8,128)(2,1)}, bf16[1,64,1280]{2,1,0:T(8,128)(2,1)}) custom-call(bf16[128,1280]{1,0:T(8,128)(2,1)} %get-tuple-element.4.prompt, bf16[1,64,1280]{2,1,0:T(8,128)(2,1)} %bitcast.5), custom_call_target="tpu_custom_call" | custom-call | tf_op jit(solution)/shard_map/pallas_call | solution.py:404
